TPU v7x, 256 devices: a whole 4x4x8 slice. The times are simulated.
256 devices in a mesh: ctx: 64 (over z, y, core), head: 4 (over x).
Axes of the slice: x: 4, y: 4, z: 8, core: 2. Of those that a mesh axis runs over, the one named last changes fastest.
Arguments:
- queries: bfloat16 [1, 8192, 2048], P(None, 'ctx', 'head'), may hold values from -24 to 24
- keys: bfloat16 [8192, 512], P('ctx', 'head'), may hold values from -6 to 6
- values: bfloat16 [8192, 512], P('ctx', 'head'), may hold values from -6 to 6
- query_pos: int32 [8192], P('ctx'), may hold values from 0 to 8191, as said below
- cot_out: bfloat16 [1, 8192, 4096], P(None, 'ctx'), may hold values from -6 to 6
- out_weight: bfloat16 [1, 2048, 4096], P(None, 'head'), may hold values from -0.09375 to 0.09375
Outputs:
- grad_queries: bfloat16 [1, 8192, 2048], P(None, 'ctx', 'head')
- grad_keys: float32 [8192, 512], P('ctx', 'head')
- grad_values: float32 [8192, 512], P('ctx', 'head')
Inputs may be any that keep to these rules, and one draw needn't show every extreme that they name: `query_pos`: the 128 rows of each index of ctx hold the consecutive positions t * 128 to t * 128 + 127 in order, and the tiles t of all indices of ctx are a permutation.
All inputs are finite; a program needn't handle non-finite values.
Results may differ from a plain program's by a relative error of at most 0.0057.
Values may be sent and summed in bfloat16 or wider, within the bound.
A program may use at most 128 MiB of HBM per device.

v0:
```python
import jax
import jax.numpy as jnp
from jax import lax
from jax.sharding import PartitionSpec as P

HEADS = 16
KV_HEADS = 4
HEAD_DIM = 128


very_negative = -1e30


def body(queries, keys, values, query_pos, cot_out, out_weight):
    layers, tile_rows, query_width = queries.shape
    kv_width = keys.shape[1]
    kv_local = kv_width // HEAD_DIM
    group_size = HEADS // KV_HEADS
    ctx_count = lax.axis_size("ctx")
    all_keys = tile_rows * ctx_count
    score_scale = HEAD_DIM ** (-0.5)
    dout = jnp.einsum(
        "ltd,led->lte", cot_out, out_weight, preferred_element_type=jnp.float32
    ).astype(jnp.bfloat16)
    query_rows = (
        queries.reshape(layers, tile_rows, kv_local, group_size, HEAD_DIM)
        .transpose(2, 0, 3, 1, 4)
        .reshape(kv_local, -1, HEAD_DIM)
    )
    dout_rows = (
        dout.reshape(layers, tile_rows, kv_local, group_size, HEAD_DIM)
        .transpose(2, 0, 3, 1, 4)
        .reshape(kv_local, -1, HEAD_DIM)
    )
    row_pos = jnp.tile(query_pos, layers * group_size)
    row_count = query_rows.shape[1]

    def head_scores(kv_head, key_piece, value_piece):
        score = (
            jnp.einsum(
                "rd,kd->rk", query_rows[kv_head], key_piece, preferred_element_type=jnp.float32
            )
            * score_scale
        )
        grad_prob = jnp.einsum(
            "rd,kd->rk", dout_rows[kv_head], value_piece, preferred_element_type=jnp.float32
        )
        key_index = jnp.arange(key_piece.shape[0], dtype=jnp.int32)
        visible = key_index[None, :] <= row_pos[:, None]
        return (score, grad_prob, visible, key_piece)

    def make_grads_step(log_total, delta):

        def grads_step(state_now, pieces, begin_row):
            key_piece, value_piece = pieces
            score, grad_prob, visible, key_head = head_scores(0, key_piece, value_piece)
            prob = jnp.where(visible, jnp.exp(score - log_total[0][:, None]), 0.0)
            grad_score = (prob * (grad_prob - delta[0][:, None])).astype(jnp.bfloat16)
            prob_low = prob.astype(jnp.bfloat16)
            query_parts = [jnp.dot(grad_score, key_head, preferred_element_type=jnp.float32)]
            key_parts = jnp.einsum(
                "rk,rd->kd", grad_score, query_rows[0], preferred_element_type=jnp.float32
            )
            value_parts = jnp.einsum(
                "rk,rd->kd", prob_low, dout_rows[0], preferred_element_type=jnp.float32
            )
            return (jnp.stack(query_parts), key_parts, value_parts)

        return grads_step

    grads_initial = (
        jnp.zeros((kv_local, row_count, HEAD_DIM), jnp.float32),
        jnp.zeros((all_keys, kv_width), jnp.float32),
        jnp.zeros((all_keys, kv_width), jnp.float32),
    )
    key_piece = lax.all_gather(keys, "ctx", axis=0, tiled=True)
    value_piece = lax.all_gather(values, "ctx", axis=0, tiled=True)
    row_tops = jnp.full((kv_local, row_count), very_negative, jnp.float32)
    row_sums = jnp.zeros((kv_local, row_count), jnp.float32)
    row_cross = jnp.zeros((kv_local, row_count), jnp.float32)
    kv_head = 0
    score, grad_prob, visible, key_head = head_scores(kv_head, key_piece, value_piece)
    score = jnp.where(visible, score, very_negative)
    top_now = jnp.maximum(row_tops[kv_head], jnp.max(score, axis=1))
    rescale = jnp.exp(row_tops[kv_head] - top_now)
    weight = jnp.where(visible, jnp.exp(score - top_now[:, None]), 0.0)
    new_tops = [top_now]
    new_sums = [row_sums[kv_head] * rescale + jnp.sum(weight, axis=1)]
    new_cross = [row_cross[kv_head] * rescale + jnp.sum(weight * grad_prob, axis=1)]
    row_tops = jnp.stack(new_tops)
    row_sums = jnp.stack(new_sums)
    row_cross = jnp.stack(new_cross)
    grads_step = make_grads_step(row_tops + jnp.log(row_sums), row_cross / row_sums)
    grad_query, key_terms, value_terms = grads_step(
        grads_initial,
        (
            lax.all_gather(keys, "ctx", axis=0, tiled=True),
            lax.all_gather(values, "ctx", axis=0, tiled=True),
        ),
        jnp.int32(0),
    )
    grad_keys, grad_values = (
        lax.psum_scatter(key_terms * score_scale, "ctx", scatter_dimension=0, tiled=True),
        lax.psum_scatter(value_terms, "ctx", scatter_dimension=0, tiled=True),
    )
    grad_queries = (grad_query * score_scale).astype(jnp.bfloat16)
    grad_queries = (
        grad_queries.reshape(kv_local, layers, group_size, tile_rows, HEAD_DIM)
        .transpose(1, 3, 0, 2, 4)
        .reshape(layers, tile_rows, query_width)
    )
    return (grad_queries, grad_keys, grad_values)


def solution(mesh):
    in_specs = (
        P(None, "ctx", "head"),
        P("ctx", "head"),
        P("ctx", "head"),
        P("ctx"),
        P(None, "ctx", None),
        P(None, "head", None),
    )
    out_specs = (P(None, "ctx", "head"), P("ctx", "head"), P("ctx", "head"))
    return jax.shard_map(body, mesh=mesh, in_specs=in_specs, out_specs=out_specs, check_vma=False)
```

profile of v0, /device:TPU:1, one launch (start us, length us, event | category | flops | bytes accessed | tf_op | source)
XLA Modules:
  0.0 486.6 jit_solution(10956002976650577480)
XLA Ops:
  7.2 0.0 copy-start
  7.2 0.0 all-gather.3.cloned.1.call-start
  7.2 0.7 all-gather.3.cloned.1.call-update
  7.9 0.0 all-gather.5.cloned.1.call-start
  8.0 0.7 all-gather.5.cloned.1.call-update
  8.7 0.0 reduce-scatter.5.cloned.1.call-start
  8.7 1.0 copy.12
  9.7 0.1 copy.13
  9.9 0.0 copy-done
  9.9 3.7 fusion.9
  13.7 0.7 broadcast_bitcast_fusion
  14.3 78.0 %all-gather.3.cloned.1.call-done = bf16[8192,128]{1,0:T(8,128)(2,1)} async-done(((bf16[128,128]{1,0:T(8,128)(2,1)}), bf16[8192,128]{1,0:T(8,128)(2,1)}) %all-gather.3.cloned.1.call-update) | async-done | bytes 2097168 | tf_op jit(solution)/shard_map/all_gather | solution.py:97
  92.3 9.0 %fusion.1 = (f32[512]{0:T(512)S(1)}, f32[512,8192]{1,0:T(8,128)}) fusion(s32[512]{0:T(512)S(1)} %broadcast_bitcast_fusion, bf16[512,128]{1,0:T(8,128)(2,1)S(1)} %bitcast.31, bf16[8192,128]{1,0:T(8,128)(2,1)} %all-gather.3.cloned.1.call-done), kind=kOutput, calls=%fused_computation.6 | convolution fusion | flops 1090518528 | bytes 19009536 | tf_op jit(solution)/shard_map/rd,kd->rk/dot_general | solution.py:40
  101.3 68.8 %all-gather.5.cloned.1.call-done = bf16[8192,128]{1,0:T(8,128)(2,1)} async-done(((bf16[128,128]{1,0:T(8,128)(2,1)}), bf16[8192,128]{1,0:T(8,128)(2,1)}) %all-gather.5.cloned.1.call-update) | async-done | bytes 2097168 | tf_op jit(solution)/shard_map/all_gather | solution.py:98
  170.1 14.1 %fusion.3 = (f32[512]{0:T(512)S(1)}, f32[512]{0:T(512)S(1)}, f32[512,8192]{1,0:T(8,128)}) fusion(f32[512,8192]{1,0:T(8,128)} %get-tuple-element.8, f32[512]{0:T(512)S(1)} %broadcast_maximum_fusion, s32[512]{0:T(512)S(1)} %broadcast_bitcast_fusion, bf16[512,128]{1,0:T(8,128)(2,1)S(1)} %bitcast.34, bf16[8192,128]{1,0:T(8,128)(2,1)} %all-gather.5.cloned.1.call-done), kind=kOutput, calls=%fused_computation.9 | convolution fusion | flops 1107295232 | bytes 35790848 | tf_op jit(solution)/shard_map/rd,kd->rk/dot_general | solution.py:45
  184.2 12.3 %fusion.4 = f32[8192,128]{1,0:T(8,128)} fusion(bf16[512,128]{1,0:T(8,128)(2,1)S(1)} %bitcast.35, f32[512,8192]{1,0:T(8,128)} %get-tuple-element.8, f32[512]{0:T(512)S(1)} %get-tuple-element.5, s32[512]{0:T(512)S(1)} %broadcast_bitcast_fusion), kind=kOutput, calls=%fused_computation.10 | convolution fusion | flops 1094713344 | bytes 21106688 | tf_op jit(solution)/shard_map/rk,rd->kd/dot_general | solution.py:64
  196.5 0.0 reduce-scatter.5.cloned.1.call-update
  196.6 0.2 reduce-scatter.3.cloned.1.call-start
  196.8 12.4 %multiply_convert_fusion = bf16[512,8192]{1,0:T(8,128)(2,1)S(1)} fusion(f32[512,8192]{1,0:T(8,128)} %get-tuple-element.9, f32[512,8192]{1,0:T(8,128)} %get-tuple-element.8, f32[512]{0:T(512)S(1)} %get-tuple-element.6, f32[512]{0:T(512)S(1)} %get-tuple-element.5, s32[512]{0:T(512)S(1)} %broadcast_bitcast_fusion), kind=kLoop, calls=%fused_computation | loop fusion | flops 29360128 | bytes 41949184 | tf_op jit(solution)/shard_map/convert_element_type | solution.py:58
  209.2 0.0 copy-start.1
  209.2 3.2 copy-done.1
  212.4 0.0 copy-start.2
  212.4 4.3 convolution_multiply_fusion
  216.7 0.0 reduce-scatter.3.cloned.1.call-update
  216.8 0.0 copy-done.2
  216.8 5.8 %fusion.8 = bf16[512,128]{1,0:T(8,128)(2,1)S(1)} fusion(bf16[512,8192]{1,0:T(8,128)(2,1)} %copy-done.1, bf16[8192,128]{1,0:T(8,128)(2,1)S(1)} %copy-done.2), kind=kOutput, calls=%fused_computation.14 | convolution fusion | flops 1073872896 | bytes 10616832 | tf_op jit(solution)/shard_map/dot_general | solution.py:60
  222.6 0.1 copy.15
  222.7 0.7 reshape.66
  223.4 109.3 %reduce-scatter.5.cloned.1.call-done = f32[128,128]{1,0:T(8,128)} async-done(((f32[8192,128]{1,0:T(8,128)}), f32[128,128]{1,0:T(8,128)}) %reduce-scatter.5.cloned.1.call-update) | async-done | bytes 65552 | tf_op jit(solution)/shard_map/reduce_scatter | solution.py:104
  332.7 147.3 %reduce-scatter.3.cloned.1.call-done = f32[128,128]{1,0:T(8,128)} async-done(((f32[8192,128]{1,0:T(8,128)}), f32[128,128]{1,0:T(8,128)}) %reduce-scatter.3.cloned.1.call-update) | async-done | bytes 65552 | tf_op jit(solution)/shard_map/reduce_scatter | solution.py:103
  (4 shorter events, 0.1 us)
Async XLA Ops:
  7.2 2.7 copy-start
  7.2 85.2 %all-gather.3.cloned.1.call-start = ((), (), s32[]{:S(2)}) async-start(), calls=%async_computation.2 | async-start | bytes 2129920 | tf_op jit(solution)/shard_map/all_gather | solution.py:97
  7.9 162.2 %all-gather.5.cloned.1.call-start = ((), (), s32[]{:S(2)}) async-start(), calls=%async_computation.3 | async-start | bytes 2129920 | tf_op jit(solution)/shard_map/all_gather | solution.py:98
  8.7 324.1 %reduce-scatter.5.cloned.1.call-start = ((), (), s32[]{:S(2)}) async-start(), calls=%async_computation.5 | async-start | bytes 4259840 | tf_op jit(solution)/shard_map/reduce_scatter | solution.py:104
  196.6 283.5 %reduce-scatter.3.cloned.1.call-start = ((), (), s32[]{:S(2)}) async-start(), calls=%async_computation.4 | async-start | bytes 4259840 | tf_op jit(solution)/shard_map/reduce_scatter | solution.py:103
  209.2 3.2 copy-start.1
  212.4 4.4 copy-start.2
Sparse Core Ops, SparseCore 0:
  10.8 81.5 all-gather.2
  95.1 74.9 all-gather.4
  196.7 135.9 reduce-scatter.4
  337.8 142.1 reduce-scatter.2
where the time goes:
time: 491 us; the launch traced here: 487 us
  waiting for transfers between devices  405 us (82%)
  matrix products  49.3 us (10%)
  between operations  13.8 us (3%)
  other arithmetic  12.4 us (3%)
  local copies, waits for them, and re-layouts  5.92 us (1%)
    reduce_scatter x1, waiting for transfers between devices, body(): lax.psum_scatter(key_terms * score_scale, 'ctx', scatter_dimension=0, til...  147 us
    reduce_scatter x1, waiting for transfers between devices, body(): lax.psum_scatter(value_terms, 'ctx', scatter_dimension=0, tiled=True)  109 us
    all_gather x1, waiting for transfers between devices, body(): lax.all_gather(keys, 'ctx', axis=0, tiled=True)  78 us
    all_gather x1, waiting for transfers between devices, body(): lax.all_gather(values, 'ctx', axis=0, tiled=True)  68.8 us
    dot_general x1, matrix products, head_scores(): jnp.einsum('rd,kd->rk', dout_rows[kv_head], value_piece, preferred_elemen...  14.1 us
    convert_element_type x1, other arithmetic, grads_step(): grad_score = (prob * (grad_prob - delta[0][:, None])).astype(jnp.bfloat16)  12.4 us
    dot_general x1, matrix products, grads_step(): jnp.einsum('rk,rd->kd', prob_low, dout_rows[0], preferred_element_type=jn...  12.3 us
  transfers between devices with their start and end apart: 4, of which 4 were waited for; matrix products, arithmetic and copies ran while one was open for 8% of the time, Pallas kernels for 0%

commit v1 on v0

v1 whole, which is shorter than its diff:
```python
import jax
import jax.numpy as jnp
import numpy as np
from jax import lax
from jax.experimental import pallas as pl
from jax.experimental.pallas import tpu as pltpu
from jax.sharding import PartitionSpec as P

HEAD_DIM = 128
GROUP = 4
TILE = 128
ZS, YS, CORES = 8, 4, 2
CHUNK = CORES * TILE
ROWS = YS * TILE
MODEL = 4096
SCALE = HEAD_DIM**-0.5
SCALE_LOG2 = float(SCALE * np.log2(np.e))
HIDDEN = -1e30
FLOOR = -1e20
BF, F32, I32 = jnp.bfloat16, jnp.float32, jnp.int32
MESH = pl.DeviceIdType.MESH
VM = pltpu.VMEM
COPIES = 80


def nt(a, b):
    return lax.dot_general(a, b, (((1,), (1,)), ((), ())), preferred_element_type=F32)


def nn(a, b):
    return lax.dot_general(a, b, (((1,), (0,)), ((), ())), preferred_element_type=F32)


def tn(a, b):
    return lax.dot_general(a, b, (((0,), (0,)), ((), ())), preferred_element_type=F32)


def kernel(
    q_hbm, k_hbm, v_hbm, pos_hbm, cot_hbm, w_hbm,
    g_ref,
    wbuf, cbuf, pos_s, qbuf, dobuf, kv, tbuf, pst, dpst, mstat, lstat, xstat, st, tot,
    acc, dq_acc, sib_out, sib_in, ring_out, relay_in, near_in, dq_out, dq_in,
    lsem, ssem, rsem,
):
    me = lax.axis_index("ctx")
    core = me % 2
    y = (me // 2) % YS
    z = me // (2 * YS)

    def at(dz=0, dy=0, other=False):
        zz = (z + dz + ZS) % ZS
        yy = (y + dy + YS) % YS
        cc = 1 - core if other else core
        return (zz * YS + yy) * 2 + cc

    zr, zl, yr, yl, yo, sib = at(dz=1), at(dz=-1), at(dy=1), at(dy=-1), at(dy=2), at(other=True)

    used = [0, 0]
    sends = []

    def send(src, dst, dev):
        i = used[0]
        used[0] += 1
        d = pltpu.make_async_remote_copy(
            src_ref=src, dst_ref=dst, send_sem=ssem.at[i], recv_sem=rsem.at[i],
            device_id={"ctx": dev}, device_id_type=MESH,
        )
        d.start()
        sends.append(d)
        return d

    def local(src, dst):
        i = used[1]
        used[1] += 1
        d = pltpu.make_async_copy(src, dst, lsem.at[i])
        d.start()
        return d

    own_kv = [local(k_hbm, kv.at[0, 0, 0]), local(v_hbm, kv.at[0, 0, 1])]
    own_pos = local(pos_hbm, pos_s)
    own_q = [local(q_hbm.at[0, :, pl.ds(h * 128, 128)], qbuf.at[h, 0]) for h in range(GROUP)]
    own_c = local(cot_hbm.at[0], cbuf)
    own_w = [local(w_hbm.at[0, pl.ds(i * 256, 256)], wbuf.at[i]) for i in range(2)]

    barrier = pltpu.get_barrier_semaphore()
    greeted = (zr, zl, at(dz=2), at(dz=-2), yr, yl, yo, sib)
    for dev in greeted:
        pl.semaphore_signal(barrier, inc=1, device_id={"ctx": dev}, device_id_type=MESH)

    own_c.wait()
    for i in range(2):
        own_w[i].wait()
        out = nt(cbuf[...], wbuf[i])
        for j in range(2):
            dobuf[2 * i + j, 0] = out[:, j * 128 : (j + 1) * 128].astype(BF)
    for d in own_kv + own_q:
        d.wait()
    own_pos.wait()
    tbuf[0] = jnp.full((8, 128), pos_s[0], I32)
    pl.semaphore_wait(barrier, len(greeted))

    def to_y(src, dst):
        return [send(src, dst(3), yr), send(src, dst(1), yl), send(src, dst(2), yo)]

    kv_sib = {0: send(kv.at[0, 0], kv.at[0, 1], sib)}
    kv_in = {
        7: [send(kv.at[0, 0], kv.at[7, 0], zr)],
        1: [send(kv.at[0, 0], kv.at[1, 0], zl)],
        6: [send(kv.at[0, 0], kv.at[6, 0], at(dz=2))],
        2: [send(kv.at[0, 0], kv.at[2, 0], at(dz=-2))],
    }
    t_in = to_y(tbuf.at[0], lambda n: tbuf.at[n])
    q_in = to_y(qbuf.at[:, 0], lambda n: qbuf.at[:, n])
    do_in = to_y(dobuf.at[:, 0], lambda n: dobuf.at[:, n])

    def arrive(n):
        for d in kv_in[n]:
            d.wait_recv()
        kv_sib[n] = send(kv.at[n, 0], kv.at[n, 1], sib)

    def relay():
        arrive(6)
        kv_in[5] = [send(kv.at[6, 0], kv.at[5, 0], zr)]
        kv_in[4] = [send(kv.at[6, 0, 0], kv.at[4, 0, 0], at(dz=2))]
        arrive(2)
        kv_in[3] = [send(kv.at[2, 0], kv.at[3, 0], zl)]
        kv_in[4].append(send(kv.at[2, 0, 1], kv.at[4, 0, 1], at(dz=-2)))

    lane = lax.broadcasted_iota(I32, (1, 128), 1)
    krow = lax.broadcasted_iota(I32, (TILE, 128), 0)

    def stat_row(h, dy):
        return ((y + dy) % YS) * GROUP + h

    def score_pass(dz):
        base = [(((z + dz) % ZS * YS + y) * 2 + c) * TILE for c in (core, 1 - core)]

        def step(h, _):
            keys = kv[dz, :, 0].reshape(CHUNK, HEAD_DIM)
            s = nt(keys, qbuf[h].reshape(ROWS, HEAD_DIM))
            for dy in range(YS):
                pos = tbuf[dy][0:1, :] + lane
                parts = []
                for c in range(2):
                    part = s[c * TILE : (c + 1) * TILE, dy * 128 : (dy + 1) * 128] * SCALE_LOG2
                    parts.append(jnp.where(krow <= pos - base[c], part, HIDDEN))
                top = jnp.maximum(
                    jnp.max(jnp.maximum(parts[0], parts[1]), axis=0, keepdims=True), FLOOR
                )
                total = jnp.zeros((TILE, 128), F32)
                for c in range(2):
                    e = jnp.exp2(parts[c] - top)
                    pst[dz, h, c * TILE : (c + 1) * TILE, dy * 128 : (dy + 1) * 128] = e
                    total = total + e
                row = stat_row(h, dy)
                mstat[dz, pl.ds(row, 1), :] = top
                lstat[dz, pl.ds(row, 1), :] = jnp.sum(total, axis=0, keepdims=True)
            return 0

        for h in range(GROUP):
            step(h, 0)

    def cross_pass(dz):
        def step(h, _):
            vals = kv[dz, :, 1].reshape(CHUNK, HEAD_DIM)
            dp = nt(vals, dobuf[h].reshape(ROWS, HEAD_DIM))
            dpst[dz, h] = dp
            cross = jnp.sum(dp * pst[dz, h], axis=0, keepdims=True)
            for dy in range(YS):
                xstat[dz, pl.ds(stat_row(h, dy), 1), :] = cross[:, dy * 128 : (dy + 1) * 128]
            return 0

        for h in range(GROUP):
            step(h, 0)

    for n in (1, 7):
        arrive(n)
    for d in q_in + t_in:
        d.wait_recv()
    kv_sib[0].wait_recv()
    relay()
    score_pass(0)
    for n in (1, 7, 2, 6):
        kv_sib[n].wait_recv()
        score_pass(n)
    for d in do_in:
        d.wait_recv()
    for n in (0, 1, 7):
        cross_pass(n)
    arrive(3)
    arrive(5)
    cross_pass(2)
    cross_pass(6)
    for n in (3, 5):
        kv_sib[n].wait_recv()
        score_pass(n)
    arrive(4)
    cross_pass(3)
    cross_pass(5)
    kv_sib[4].wait_recv()
    score_pass(4)
    cross_pass(4)

    top = mstat[0]
    for i in range(1, ZS):
        top = jnp.maximum(top, mstat[i])
    total, cross = jnp.zeros_like(top), jnp.zeros_like(top)
    for i in range(ZS):
        w = jnp.exp2(mstat[i] - top)
        total = total + lstat[i] * w
        cross = cross + xstat[i] * w
    st[0, 0], st[0, 1], st[0, 2] = top, total, cross
    for d in to_y(st.at[0], lambda n: st.at[n]):
        d.wait_recv()
    top = jnp.maximum(jnp.maximum(st[0, 0], st[1, 0]), jnp.maximum(st[2, 0], st[3, 0]))
    total, cross = jnp.zeros_like(top), jnp.zeros_like(top)
    for i in range(YS):
        w = jnp.exp2(st[i, 0] - top)
        total = total + st[i, 1] * w
        cross = cross + st[i, 2] * w
    tot[0] = top + jnp.log2(total)
    tot[1] = cross / total

    def grad_pass(dz, heads, first, dq_first):
        keys = kv[dz, :, 0].reshape(CHUNK, HEAD_DIM)
        dk, dv = [], []
        for h in heads:
            rows = [stat_row(h, dy) for dy in range(YS)]
            factor = jnp.concatenate(
                [jnp.exp2(mstat[dz, pl.ds(r, 1), :] - tot[0, pl.ds(r, 1), :]) for r in rows], axis=1
            )
            delta = jnp.concatenate([tot[1, pl.ds(r, 1), :] for r in rows], axis=1)
            prob = pst[dz, h] * factor
            ds = (prob * (dpst[dz, h] - delta)).astype(BF)
            prob = prob.astype(BF)
            dv_now = nn(prob, dobuf[h].reshape(ROWS, HEAD_DIM))
            dk_now = nn(ds, qbuf[h].reshape(ROWS, HEAD_DIM))
            if first and h == heads[0]:
                acc[dz, 0], acc[dz, 1] = dk_now, dv_now
            else:
                acc[dz, 0] += dk_now
                acc[dz, 1] += dv_now
            dq = tn(keys, ds)
            if dq_first:
                dq_acc[h] = dq
            else:
                dq_acc[h] += dq

    sib_copies = {}

    def to_sib(dz):
        for i in range(2):
            sib_out[dz, i] = acc[dz, i, TILE:].astype(BF)
        sib_copies[dz] = send(sib_out.at[dz], sib_in.at[dz], sib)

    def pair(dz):
        sib_copies[dz].wait_recv()
        return [acc[dz, i, :TILE] + sib_in[dz, i].astype(F32) for i in range(2)]

    def to_owner(dz, parts):
        ring_out[dz, 0], ring_out[dz, 1] = parts[0].astype(BF), parts[1].astype(BF)

    every = tuple(range(GROUP))
    grad_pass(4, every, True, True)
    to_sib(4)
    grad_pass(3, every, True, False)
    to_sib(3)
    to_owner(4, pair(4))
    far = [
        send(ring_out.at[4, 0], relay_in.at[0, 0], at(dz=2)),
        send(ring_out.at[4, 1], relay_in.at[1, 1], at(dz=-2)),
    ]
    grad_pass(5, every, True, False)
    to_sib(5)
    to_owner(3, pair(3))
    three = [send(ring_out.at[3], relay_in.at[2], zr)]
    rest = (2, 6, 1, 7, 0)
    for n in rest:
        grad_pass(n, (0, 1), True, False)
        if n == 2:
            to_owner(5, pair(5))
            three.append(send(ring_out.at[5], relay_in.at[3], zl))

    def send_dq(half):
        for dy in range(1, YS):
            for h in half:
                dq_out[dy, h] = dq_acc[h, :, dy * 128 : (dy + 1) * 128].astype(BF)
        cut = pl.ds(half[0], 2)
        return [
            send(dq_out.at[2, cut], dq_in.at[2, cut], yo),
            send(dq_out.at[1, cut], dq_in.at[3, cut], yr),
            send(dq_out.at[3, cut], dq_in.at[1, cut], yl),
        ]

    dq_copies = send_dq((0, 1))
    for n in rest:
        grad_pass(n, (2, 3), False, False)
        to_sib(n)
        if n == 6:
            for d in far + three:
                d.wait_recv()
            gk, gv = pair(2)
            to_owner(2, (gk + relay_in[0, 0].astype(F32) + relay_in[2, 0].astype(F32), gv + relay_in[2, 1].astype(F32)))
            near = [send(ring_out.at[2], near_in.at[0], at(dz=2))]
        if n == 1:
            gk, gv = pair(6)
            to_owner(6, (gk + relay_in[3, 0].astype(F32), gv + relay_in[1, 1].astype(F32) + relay_in[3, 1].astype(F32)))
            near.append(send(ring_out.at[6], near_in.at[1], at(dz=-2)))
        if n == 7:
            to_owner(1, pair(1))
            near.append(send(ring_out.at[1], near_in.at[2], zr))
    dq_copies += send_dq((2, 3))
    to_owner(7, pair(7))
    near.append(send(ring_out.at[7], near_in.at[3], zl))
    gk, gv = pair(0)
    for d in near:
        d.wait_recv()
    for i in range(4):
        gk = gk + near_in[i, 0].astype(F32)
        gv = gv + near_in[i, 1].astype(F32)
    g_ref[4] = gk * SCALE
    g_ref[5] = gv
    for d in dq_copies:
        d.wait_recv()
    for h in range(GROUP):
        g = dq_acc[h, :, 0:128]
        for n in range(1, YS):
            g = g + dq_in[n, h].astype(F32)
        g_ref[h] = g * SCALE

    for d in sends:
        d.wait_send()
    assert used[0] <= COPIES and used[1] <= 16


def write_out(g_ref, gq_ref, gk_ref, gv_ref):
    for h in range(GROUP):
        gq_ref[0, :, h * 128 : (h + 1) * 128] = g_ref[h].T.astype(BF)
    gk_ref[...] = g_ref[4]
    gv_ref[...] = g_ref[5]


def body(queries, keys, values, query_pos, cot_out, out_weight):
    any_ = pl.BlockSpec(memory_space=pl.ANY)
    vm = pl.BlockSpec(memory_space=VM)
    stat = VM((ZS, YS * GROUP, 128), F32)
    tile = (TILE, 128)
    sums = pl.pallas_call(
        kernel,
        out_shape=jax.ShapeDtypeStruct((6,) + tile, F32),
        in_specs=[any_] * 6,
        out_specs=vm,
        scratch_shapes=[
            VM((2, 256, MODEL), BF),
            VM((TILE, MODEL), BF),
            pltpu.SMEM((TILE,), I32),
            VM((GROUP, YS) + tile, BF),
            VM((GROUP, YS) + tile, BF),
            VM((ZS, 2, 2) + tile, BF),
            VM((YS, 8, 128), I32),
            VM((ZS, GROUP, CHUNK, ROWS), F32),
            VM((ZS, GROUP, CHUNK, ROWS), F32),
            stat, stat, stat,
            VM((YS, 3, YS * GROUP, 128), F32),
            VM((2, YS * GROUP, 128), F32),
            VM((ZS, 2, CHUNK, HEAD_DIM), F32),
            VM((GROUP, HEAD_DIM, ROWS), F32),
            VM((ZS, 2) + tile, BF),
            VM((ZS, 2) + tile, BF),
            VM((ZS, 2) + tile, BF),
            VM((4, 2) + tile, BF),
            VM((4, 2) + tile, BF),
            VM((YS, GROUP) + tile, BF),
            VM((YS, GROUP) + tile, BF),
            pltpu.SemaphoreType.DMA((16,)),
            pltpu.SemaphoreType.DMA((COPIES,)),
            pltpu.SemaphoreType.DMA((COPIES,)),
        ],
        compiler_params=pltpu.CompilerParams(
            collective_id=0, has_side_effects=True, vmem_limit_bytes=60 * 2**20
        ),
    )(queries, keys, values, query_pos, cot_out, out_weight)
    return pl.pallas_call(
        write_out,
        out_shape=(
            jax.ShapeDtypeStruct((1, TILE, GROUP * HEAD_DIM), BF),
            jax.ShapeDtypeStruct(tile, F32),
            jax.ShapeDtypeStruct(tile, F32),
        ),
        in_specs=[vm],
        out_specs=(vm, vm, vm),
    )(sums)


def solution(mesh):
    in_specs = (
        P(None, "ctx", "head"),
        P("ctx", "head"),
        P("ctx", "head"),
        P("ctx"),
        P(None, "ctx", None),
        P(None, "head", None),
    )
    out_specs = (P(None, "ctx", "head"), P("ctx", "head"), P("ctx", "head"))
    return jax.shard_map(body, mesh=mesh, in_specs=in_specs, out_specs=out_specs, check_vma=False)
```

time: 491 us -> 54.8 us (0.11)
  waiting for transfers between devices: 405 us -> 0 us
  Pallas kernels: 0 us -> 54.1 us
  matrix products: 49.3 us -> 0 us
  between operations: 13.8 us -> 0.64 us
  other arithmetic: 12.4 us -> 0 us
  local copies, waits for them, and re-layouts: 5.92 us -> 0 us
    reduce_scatter x2 -> x0, waiting for transfers between devices: 257 us -> none  [the longest x1 147 us: body(): lax.psum_scatter(key_terms * score_scale, 'ctx', scatter_dimension=0, til...]
    all_gather x2 -> x0, waiting for transfers between devices: 147 us -> none  [the longest x1 78 us: body(): lax.all_gather(keys, 'ctx', axis=0, tiled=True)]
    pallas_call x0 -> x2, Pallas kernels: none -> 54.1 us  [the longest x1 52.3 us: body(): pl.pallas_call(kernel, out_shape=jax.ShapeDtypeStruct((6,) + tile, F32),...]
    dot_general x6 -> x0, matrix products: 49.3 us -> none  [the longest x1 14.1 us: head_scores(): jnp.einsum('rd,kd->rk', dout_rows[kv_head], value_piece, preferred_elemen...]
    convert_element_type x1 -> x0, other arithmetic: 12.4 us -> none  [grads_step(): grad_score = (prob * (grad_prob - delta[0][:, None])).astype(jnp.bfloat16)]
  transfers between devices with their start and end apart: 4 -> 0, of which waited for: 4 -> 0; matrix products, arithmetic and copies ran while one was open for 8% -> 0% of each run, Pallas kernels for 0% -> 0%
where the time goes in v1:
time: 54.8 us; the launch traced here: 54.7 us
  Pallas kernels  54.1 us (99%)
  between operations  0.64 us (1%)
    pallas_call x1, Pallas kernels, body(): pl.pallas_call(kernel, out_shape=jax.ShapeDtypeStruct((6,) + tile, F32),...  52.3 us
    pallas_call x1, Pallas kernels, body(): pl.pallas_call(write_out, out_shape=(jax.ShapeDtypeStruct((1, TILE, GROUP...  1.76 us

profile of v1, /device:TPU:1, one launch (start us, length us, event | category | flops | bytes accessed | tf_op | source)
XLA Modules:
  0.0 54.7 jit_solution(1271992302501940880)
XLA Ops:
  0.6 52.3 %shard_map.85.g_ref = f32[6,128,128]{2,1,0:T(8,128)} custom-call(bf16[1,128,512]{2,1,0:T(8,128)(2,1)} %q_hbm.1, bf16[128,128]{1,0:T(8,128)(2,1)} %k_hbm.1, bf16[128,128]{1,0:T(8,128)(2,1)} %v_hbm.1, s32[128]{0:T(128)} %pos_hbm.1, bf16[1,128,4096]{2,1,0:T(8,128)(2,1)} %cot_hbm.1, bf16[1,512,4096]{2,1,0:T(8,128)(2,1)} %w_hbm.1), custom_call_target="tpu_custom_call" | custom-call | tf_op jit(solution)/shard_map/pallas_call | solution.py:348
  53.0 1.8 %shard_map.86 = (bf16[1,128,512]{2,1,0:T(8,128)(2,1)}, f32[128,128]{1,0:T(8,128)}, f32[128,128]{1,0:T(8,128)}) custom-call(f32[6,128,128]{2,1,0:T(8,128)} %shard_map.85.g_ref), custom_call_target="tpu_custom_call" | custom-call | tf_op jit(solution)/shard_map/pallas_call | solution.py:383
